TPU v7x, 32 devices: a whole 2x2x4 slice. The times are simulated.
32 devices in a mesh: row: 4 (over y, core), col: 8 (over z, x).
Axes of the slice: x: 2, y: 2, z: 4, core: 2. Of those that a mesh axis runs over, the one named last changes fastest.
Arguments:
- points: float32 [16, 16384], P(None, ('row', 'col')), may hold values from -0.125 to 1.125
- lengthscale: float32 [16], replicated, may hold values from 2 to 6, as said below
- noise_var: float32 [128], replicated, may hold values from 0.2 to 2
- groups: int32 [32], replicated, may hold values from 0 to 63
- targets: float32 [16384, 128], P(('row', 'col')), may hold values from -162 to 162, as said below
Outputs:
- solution_field: float32 [16384, 128], P(('row', 'col'))
- residual: float32 [16384, 128], P(('row', 'col'))
Inputs may be any that keep to these rules, and one draw needn't show every extreme that they name: Observed targets, real-valued. `lengthscale`: length scales, positive.
All inputs are finite; a program needn't handle non-finite values.
Results may differ from a plain program's by a relative error of at most 0.029.
Values may be sent and summed in bfloat16 or wider, within the bound.
A program may use at most 64 MiB of HBM per device.

v0:
```python
import functools

import functools

import jax
import jax.numpy as jnp
from jax import lax
from jax.experimental import pallas as pl
from jax.experimental.pallas import tpu as pltpu
from jax.sharding import PartitionSpec as P

TILE = 512
ITERS = 2
RHS = 128
CHUNK = 128
GATHER_LIMIT = 64
KEPT = 32
VMEM_LIMIT = 24 * 1024 * 1024
MESH = pl.DeviceIdType.MESH


def split3(value):
    first = value.astype(jnp.bfloat16).astype(jnp.float32)
    rest = value - first
    second = rest.astype(jnp.bfloat16).astype(jnp.float32)
    return first, second, rest - second


def lifted(coords, factor, norm_at, one_at):
    wide = coords.astype(jnp.float32)
    parts = split3(jnp.sum(wide * wide, axis=0, keepdims=True))
    row = lax.broadcasted_iota(jnp.int32, wide.shape, 0)
    tail = jnp.where((row >= one_at) & (row < one_at + 3), 1.0, 0.0)
    for place, part in enumerate(parts):
        tail = jnp.where(row == norm_at + place, part, tail)
    return jnp.concatenate([wide * factor, tail], axis=0).astype(jnp.bfloat16)


def wendland(squared):
    safe = jnp.maximum(squared, 1e-30)
    radius = safe * lax.rsqrt(safe)
    support = jnp.maximum(1.0 - radius, 0.0)
    second = support * support
    third = second * support
    fourth = second * second
    eighth = fourth * fourth
    return ((eighth * third) * (12.0 - 11.0 * support)).astype(jnp.bfloat16)


def place():
    row, col = lax.axis_index("row"), lax.axis_index("col")
    return row // 2, lax.rem(row, 2), col // 2, lax.rem(col, 2)


def device(y, core, z, x):
    return (2 * y + core, 2 * z + x)


def greet(targets):
    barrier = pltpu.get_barrier_semaphore()
    for target in targets:
        pl.semaphore_signal(barrier, inc=1, device_id=target, device_id_type=MESH)


def greeted(targets):
    pl.semaphore_wait(pltpu.get_barrier_semaphore(), len(targets))


class Plane:
    def __init__(self, n_col, out, send_sems, recv_sems):
        self.out, self.send_sems, self.recv_sems = out, send_sems, recv_sems
        self.y, self.core, self.z, self.x = place()
        self.depth = n_col // 2
        self.started = []
        y, core, z, x = self.y, self.core, self.z, self.x
        self.over_x, self.over_y = device(y, core, z, 1 - x), device(1 - y, core, z, x)
        self.over_core = device(y, 1 - core, z, x)
        self.partners = [self.over_x, self.over_y, self.over_core]
        self.partners += [self.over_z(step) for step in range(1, self.depth)]

    def level(self, step):
        return lax.rem(self.z + step, self.depth)

    def over_z(self, step):
        return device(self.y, self.core, self.level(self.depth - step), self.x)

    def launch(self, source, spot, recv_sem, target):
        copy = pltpu.make_async_remote_copy(
            src_ref=source,
            dst_ref=spot,
            send_sem=self.send_sems.at[len(self.started)],
            recv_sem=recv_sem,
            device_id=target,
            device_id_type=MESH,
        )
        copy.start()
        self.started.append(copy)

    def half(self, ref, part):
        lanes = TILE // 2
        return ref.at[:, :, pl.ds(part * lanes, lanes)]

    def spot(self, peer, steps, part):
        return self.half(self.out.at[peer, pl.ds(steps[0], steps[1])], part)

    def send(self, group, steps, peer, part, target, flip, own=None):
        source = self.spot(peer, steps, part) if own is None else self.half(own, part)
        there = peer + flip
        self.launch(source, self.spot(there, steps, part), self.recv_sems.at[group, there, part], target)

    def arrived(self, group, steps, peer, part):
        spot = self.spot(peer, steps, part)
        pltpu.make_async_copy(spot, spot, self.recv_sems.at[group, peer, part]).wait()

    def first_hop(self, group, steps, own=None):
        self.send(group, steps, 0, 0, self.over_x, 1, own)
        self.send(group, steps, 0, 1, self.over_y, 4, own)
        self.send(group, steps, 0, 1, self.over_x, 1, own)
        self.send(group, steps, 0, 0, self.over_y, 4, own)
        self.send(group, steps, 0, 0, self.over_core, 2, own)
        self.send(group, steps, 0, 1, self.over_core, 2, own)

    def second_hop(self, group, steps):
        self.arrived(group, steps, 1, 0)
        self.send(group, steps, 1, 0, self.over_y, 4)
        self.arrived(group, steps, 4, 1)
        self.send(group, steps, 4, 1, self.over_x, 1)
        self.send(group, steps, 1, 0, self.over_core, 2)
        self.send(group, steps, 4, 1, self.over_core, 2)

    def last_hop(self, group, steps):
        for peer, part in ((1, 1), (4, 0), (5, 0), (5, 1)):
            self.arrived(group, steps, peer, part)
            self.send(group, steps, peer, part, self.over_core, 2)

    def finish(self, groups):
        for group, steps in enumerate(groups):
            for peer in (2, 3, 6, 7):
                self.arrived(group, steps, peer, 0)
                self.arrived(group, steps, peer, 1)
        for copy in self.started:
            copy.wait_send()


def level_groups(depth):
    groups = [(step, 1) for step in range(min(depth, 2))]
    return groups + ([(2, depth - 2)] if depth > 2 else [])


def first_gather(n_col, points, scale, targets, out, own, send_sems, recv_sems, z_sems, own_sem):
    plane = Plane(n_col, out, send_sems, recv_sems)
    depth, dims = plane.depth, points.shape[0]
    width = targets.shape[1] // depth
    greet(plane.partners)
    across = lax.broadcasted_iota(jnp.int32, (dims, dims), 1)
    down = lax.broadcasted_iota(jnp.int32, (dims, dims), 0)
    lengths = jnp.sum(jnp.where(across == down, scale[...], 0.0), axis=1, keepdims=True)
    scaled = (points[...] / lengths).astype(jnp.bfloat16)
    turned = targets[...].T.astype(jnp.bfloat16)
    for part in range(depth):
        own[part, 0:width, :] = turned[part * width:(part + 1) * width, :]
        own[part, width:width + dims, :] = scaled
    greeted(plane.partners)
    for step in range(1, depth):
        plane.launch(own.at[plane.level(depth - step)], out.at[0, step], z_sems.at[step], plane.over_z(step))
    groups = level_groups(depth)
    for group, steps in enumerate(groups):
        if group == 0:
            mine = own.at[pl.ds(plane.z, 1)]
            plane.first_hop(0, steps, mine)
            keep = pltpu.make_async_copy(mine, out.at[0, pl.ds(0, 1)], own_sem)
            keep.start()
        else:
            for step in range(steps[0], steps[0] + steps[1]):
                spot = out.at[0, step]
                pltpu.make_async_copy(spot, spot, z_sems.at[step]).wait()
            plane.first_hop(group, steps)
            plane.second_hop(group - 1, groups[group - 1])
        if group >= 2:
            plane.last_hop(group - 2, groups[group - 2])
    last = len(groups) - 1
    plane.second_hop(last, groups[last])
    for group in range(max(last - 1, 0), last + 1):
        plane.last_hop(group, groups[group])
    keep.wait()
    plane.finish(groups)


def second_gather(n_col, own, out, back, send_sems, recv_sems, back_sems, own_sems):
    plane = Plane(n_col, out, send_sems, recv_sems)
    depth = plane.depth
    greet(plane.partners)
    keeps = [
        pltpu.make_async_copy(own, out.at[0], own_sems.at[0]),
        pltpu.make_async_copy(own.at[0], back.at[plane.z], own_sems.at[1]),
    ]
    for keep in keeps:
        keep.start()
    greeted(plane.partners)
    steps = (0, depth)
    plane.first_hop(0, steps, own)
    for step in range(1, depth):
        plane.launch(own.at[depth - step], back.at[plane.z], back_sems.at[step], plane.over_z(step))
    plane.second_hop(0, steps)
    plane.last_hop(0, steps)
    for step in range(1, depth):
        spot = back.at[plane.level(step)]
        pltpu.make_async_copy(spot, spot, back_sems.at[step]).wait()
    for keep in keeps:
        keep.wait()
    plane.finish([steps])


def finish_kernel(n_col, own, back, targets, total, once, twice,
                  land, line, wide, send_sems, recv_sems, line_sends, line_recvs, wide_sends, wide_recvs):
    y, core, z, x = place()
    depth = n_col // 2

    def level(step):
        return lax.rem(z + step, depth)

    column = [device(y, core, level(depth - step), x) for step in range(1, depth)]
    flips = [(a, b, c) for a in range(2) for b in range(2) for c in range(2)][1:]
    plane = [
        device(1 - y if a else y, 1 - core if b else core, z, 1 - x if c else x) for a, b, c in flips
    ]
    greet(column + plane)
    rhs = targets.shape[1]
    target = targets[...]
    image = back[...].reshape(rhs, TILE).astype(jnp.float32).T
    once[...] = image

    def column_sum(value):
        return jnp.sum(value, axis=0, keepdims=True)

    line[0, 0:1, :] = column_sum(target * target)
    line[0, 1:2, :] = column_sum(target * image)
    line[0, 2:3, :] = column_sum(image * image)
    line[0, 5:8, :] = jnp.zeros((3, rhs), jnp.float32)
    greeted(column + plane)

    def remote(source, spot, send_sem, recv_sem, target):
        copy = pltpu.make_async_remote_copy(
            src_ref=source, dst_ref=spot, send_sem=send_sem, recv_sem=recv_sem,
            device_id=target, device_id_type=MESH,
        )
        copy.start()
        return copy

    copies = [
        remote(own.at[depth - step], land.at[z], send_sems.at[step], recv_sems.at[step], column[step - 1])
        for step in range(1, depth)
    ]
    land[z] = own[0]
    for copy in copies:
        copy.wait()
    again = land[...].reshape(rhs, TILE).astype(jnp.float32).T
    twice[...] = again
    line[0, 3:4, :] = column_sum(target * again)
    line[0, 4:5, :] = column_sum(image * again)
    copies = [
        remote(line.at[0], line.at[step], line_sends.at[step], line_recvs.at[step], column[step - 1])
        for step in range(1, depth)
    ]
    for copy in copies:
        copy.wait()
    wide[0] = jnp.sum(line[...], axis=0)
    copies = [
        remote(wide.at[0], wide.at[step + 1], wide_sends.at[step], wide_recvs.at[step], peer)
        for step, peer in enumerate(plane)
    ]
    for copy in copies:
        copy.wait()
    total[...] = jnp.sum(wide[...], axis=0)


def find_tiles(n_col, groups, order):
    y, core, z, x = place()
    depth = n_col // 2

    def label(peer, step):
        other_y = lax.rem(y + peer // 4, 2)
        other_core = lax.rem(core + peer // 2 % 2, 2)
        other_x = lax.rem(x + peer % 2, 2)
        return groups[(2 * other_y + other_core) * n_col + 2 * lax.rem(z + step, depth) + other_x]

    labels = [label(peer, step) for peer in range(8) for step in range(depth)]
    count = jnp.int32(0)
    for level in range(depth):
        for block, other in enumerate(labels):
            order[count] = block * depth + level
            count = count + (other == labels[level]).astype(jnp.int32)
    return count


def lift_rows(n_col, width, gathered, right):
    dims = gathered.shape[1] - width
    for level in range(n_col // 2):
        right[level] = lifted(gathered[level, pl.ds(width, dims), :], 1.0, 0, 3)


def build(width, gathered, block, level, left, right, spot):
    dims = gathered.shape[1] - width
    left[...] = lifted(gathered[block, pl.ds(width, dims), :], -2.0, 3, 0).T
    for start in range(0, TILE, CHUNK):
        rows = pl.ds(start, CHUNK)
        squared = jnp.dot(left[rows, :], right[level], preferred_element_type=jnp.float32)
        spot[rows, :] = wendland(squared)


def spot_of(depth, order, slot):
    return order[slot] // depth, lax.rem(order[slot], depth)


def first_kernel(n_col, groups, gathered, tiles, narrow, order, left, right, spare, image):
    width = narrow.shape[1]
    depth, kept = n_col // 2, tiles.shape[0]
    total = find_tiles(n_col, groups, order)
    stored = jnp.minimum(total, kept)
    lift_rows(n_col, width, gathered, right)
    image[...] = jnp.zeros_like(image)

    def one_tile(slot, carry):
        block, level = spot_of(depth, order, slot)
        build(width, gathered, block, level, left, right, tiles.at[slot])
        return carry

    def multiply(slot, tile):
        block, level = spot_of(depth, order, slot)
        image[level] += jnp.dot(
            gathered[block, pl.ds(0, width), :], tile[...], preferred_element_type=jnp.float32
        )

    def one_stored(slot, carry):
        multiply(slot, tiles.at[slot])
        return carry

    def one_more(slot, carry):
        block, level = spot_of(depth, order, slot)
        build(width, gathered, block, level, left, right, spare)
        multiply(slot, spare)
        return carry

    lax.fori_loop(0, stored, one_tile, 0)
    lax.fori_loop(0, stored, one_stored, 0)
    lax.fori_loop(stored, total, one_more, 0)
    narrow[...] = image[...].astype(jnp.bfloat16)


def second_kernel(n_col, groups, gathered, source, tiles, narrow, order, left, right, spare, image):
    width = narrow.shape[1]
    depth, kept = n_col // 2, tiles.shape[0]
    total = find_tiles(n_col, groups, order)
    stored = jnp.minimum(total, kept)
    image[...] = jnp.zeros_like(image)

    def multiply(slot, tile):
        block, level = spot_of(depth, order, slot)
        image[level] += jnp.dot(source[block], tile[...], preferred_element_type=jnp.float32)

    def one_stored(slot, carry):
        multiply(slot, tiles.at[slot])
        return carry

    lax.fori_loop(0, stored, one_stored, 0)

    @pl.when(total > kept)
    def _():
        lift_rows(n_col, width, gathered, right)

    def one_more(slot, carry):
        block, level = spot_of(depth, order, slot)
        build(width, gathered, block, level, left, right, spare)
        multiply(slot, spare)
        return carry

    lax.fori_loop(stored, total, one_more, 0)
    narrow[...] = image[...].astype(jnp.bfloat16)


def gathered_plan(points, lengthscale, noise_var, groups, targets):
    n_col = lax.axis_size("col")
    depth = n_col // 2
    blocks = groups.shape[0]
    dims = points.shape[0]
    rhs = targets.shape[1]
    width = rhs // depth
    scale = lengthscale[None, :]
    variance = noise_var[None, :]
    parts = len(level_groups(depth))

    vmem = pl.BlockSpec(memory_space=pltpu.VMEM)
    smem = pl.BlockSpec(memory_space=pltpu.SMEM)
    slices = jax.ShapeDtypeStruct((depth, width, TILE), jnp.bfloat16)
    whole = jax.ShapeDtypeStruct((TILE, rhs), jnp.float32)

    def remote(number):
        return pltpu.CompilerParams(
            collective_id=number, has_side_effects=True, vmem_limit_bytes=VMEM_LIMIT
        )

    gathered = pl.pallas_call(
        functools.partial(first_gather, n_col),
        out_shape=jax.ShapeDtypeStruct((8, depth, width + dims, TILE), jnp.bfloat16),
        in_specs=[vmem, vmem, vmem],
        out_specs=vmem,
        scratch_shapes=[
            pltpu.VMEM((depth, width + dims, TILE), jnp.bfloat16),
            pltpu.SemaphoreType.DMA((depth - 1 + 14 * parts,)),
            pltpu.SemaphoreType.DMA((parts, 8, 2)),
            pltpu.SemaphoreType.DMA((depth,)),
            pltpu.SemaphoreType.DMA,
        ],
        compiler_params=remote(0),
        name="first_gather",
    )(points, scale, targets).reshape(blocks, width + dims, TILE)

    work = [
        pltpu.SMEM((depth * blocks,), jnp.int32),
        pltpu.VMEM((TILE, 2 * dims), jnp.bfloat16),
        pltpu.VMEM((depth, 2 * dims, TILE), jnp.bfloat16),
        pltpu.VMEM((TILE, TILE), jnp.bfloat16),
        pltpu.VMEM((depth, width, TILE), jnp.float32),
    ]
    tiles, first = pl.pallas_call(
        functools.partial(first_kernel, n_col),
        out_shape=[jax.ShapeDtypeStruct((KEPT, TILE, TILE), jnp.bfloat16), slices],
        in_specs=[smem, vmem],
        out_specs=[vmem, vmem],
        scratch_shapes=work,
        compiler_params=pltpu.CompilerParams(vmem_limit_bytes=VMEM_LIMIT),
        name="first_product",
    )(groups, gathered)

    source, back = pl.pallas_call(
        functools.partial(second_gather, n_col),
        out_shape=[jax.ShapeDtypeStruct((8, depth, width, TILE), jnp.bfloat16), slices],
        in_specs=[vmem],
        out_specs=[vmem, vmem],
        scratch_shapes=[
            pltpu.SemaphoreType.DMA((depth - 1 + 14,)),
            pltpu.SemaphoreType.DMA((1, 8, 2)),
            pltpu.SemaphoreType.DMA((depth,)),
            pltpu.SemaphoreType.DMA((2,)),
        ],
        compiler_params=remote(1),
        name="second_gather",
    )(first)

    second = pl.pallas_call(
        functools.partial(second_kernel, n_col),
        out_shape=slices,
        in_specs=[smem, vmem, vmem, vmem],
        out_specs=vmem,
        scratch_shapes=work,
        compiler_params=pltpu.CompilerParams(vmem_limit_bytes=VMEM_LIMIT),
        name="second_product",
    )(groups, gathered, source.reshape(blocks, width, TILE), tiles)

    total, image, again = pl.pallas_call(
        functools.partial(finish_kernel, n_col),
        out_shape=[jax.ShapeDtypeStruct((8, rhs), jnp.float32), whole, whole],
        in_specs=[vmem, vmem, vmem],
        out_specs=[vmem, vmem, vmem],
        scratch_shapes=[
            pltpu.VMEM((depth, width, TILE), jnp.bfloat16),
            pltpu.VMEM((depth, 8, rhs), jnp.float32),
            pltpu.VMEM((8, 8, rhs), jnp.float32),
        ]
        + [pltpu.SemaphoreType.DMA((depth,))] * 4
        + [pltpu.SemaphoreType.DMA((8,))] * 2,
        compiler_params=remote(2),
        name="finish",
    )(second, back, targets)

    tt, ty, yy, tz, yz = (total[place:place + 1] for place in range(5))
    step = tt / (variance * tt + ty)
    keep = 1.0 - step * variance
    after = keep * keep * tt - 2.0 * keep * step * ty + step * step * yy
    along = keep + after / tt
    squares = along * along * tt - 2.0 * along * step * ty + step * step * yy
    product = along * along * ty - along * step * (tz + yy) + step * step * yz
    second_step = after / (variance * squares + product)
    direction = along * targets - step * image
    applied = variance * direction + along * image - step * again
    solution_field = step * targets + second_step * direction
    residual = keep * targets - step * image - second_step * applied
    return (solution_field, residual)


def kernel_tile(row_coords, col_coords):
    row_norms = jnp.sum(row_coords * row_coords, axis=0)
    col_norms = jnp.sum(col_coords * col_coords, axis=0)
    crossed = lax.dot_general(
        row_coords,
        col_coords,
        (((0,), (0,)), ((), ())),
        precision=lax.Precision.HIGHEST,
        preferred_element_type=jnp.float32,
    )
    squared = jnp.maximum(row_norms[:, None] + col_norms[None, :] - 2.0 * crossed, 0.0)
    radius = jnp.sqrt(squared)
    support = jnp.maximum(1.0 - radius, 0.0)
    return (support**11 * (11.0 * radius + 1.0)).astype(jnp.bfloat16)


def per_device(points, lengthscale, noise_var, groups, targets):
    n_row = lax.axis_size("row")
    n_col = lax.axis_size("col")
    own_blocks = targets.shape[0] // TILE
    row_blocks = own_blocks * n_col
    col_blocks = own_blocks * n_row
    scaled = points / lengthscale[:, None]
    row_coords = lax.all_gather(scaled.astype(jnp.bfloat16), "col", axis=1, tiled=True).astype(
        scaled.dtype
    )
    col_coords = lax.all_gather(scaled.astype(jnp.bfloat16), "row", axis=1, tiled=True).astype(
        scaled.dtype
    )
    row_place = lax.axis_index("row")
    col_place = lax.axis_index("col")
    row_groups = lax.dynamic_slice_in_dim(groups, row_place * row_blocks, row_blocks, 0)
    col_groups = lax.dynamic_index_in_dim(
        groups.reshape(n_row, n_col, own_blocks), col_place, 1, keepdims=False
    ).reshape(col_blocks)
    flat_mask = (row_groups[:, None] == col_groups[None, :]).reshape(row_blocks * col_blocks)
    tile_count = jnp.sum(flat_mask.astype(jnp.int32))
    tile_order = jnp.nonzero(flat_mask, size=row_blocks * col_blocks, fill_value=0)[0].astype(
        jnp.int32
    )

    def square_sums(vector):
        return lax.psum(jnp.sum(vector * vector, axis=0), ("row", "col"))

    solution_field = jnp.zeros_like(targets)
    residual = targets
    direction = targets
    norm_now = square_sums(residual)
    for iteration in range(ITERS):
        narrow = direction.astype(jnp.bfloat16)
        operator_source = lax.all_gather(narrow, "row", axis=0, tiled=True)
        source = operator_source
        initial = jnp.zeros((row_blocks * TILE, RHS), jnp.float32)

        def one_tile(position, summed):
            flat_index = tile_order[position]
            row_slot = flat_index // col_blocks
            col_slot = flat_index % col_blocks
            left = lax.dynamic_slice_in_dim(row_coords, row_slot * TILE, TILE, 1)
            right = lax.dynamic_slice_in_dim(col_coords, col_slot * TILE, TILE, 1)
            values = kernel_tile(left, right)
            block_vec = lax.dynamic_slice_in_dim(source, col_slot * TILE, TILE, 0)
            product = jnp.dot(values, block_vec, preferred_element_type=jnp.float32)
            current = lax.dynamic_slice_in_dim(summed, row_slot * TILE, TILE, 0)
            return lax.dynamic_update_slice_in_dim(summed, current + product, row_slot * TILE, 0)

        partial_value = lax.fori_loop(0, tile_count, one_tile, initial)
        outgoing = partial_value.astype(jnp.bfloat16).reshape(n_col, own_blocks * TILE, RHS)
        incoming = lax.all_to_all(outgoing, "col", split_axis=0, concat_axis=0, tiled=True)
        operator_product = jnp.sum(incoming, axis=0, dtype=jnp.float32)
        image = noise_var[None, :] * direction + operator_product
        curve = lax.psum(jnp.sum(direction * image, axis=0), ("row", "col"))
        step_size = norm_now / curve
        solution_field = solution_field + step_size[None, :] * direction
        residual = residual - step_size[None, :] * image
        if iteration + 1 < ITERS:
            norm_next = square_sums(residual)
            direction = residual + (norm_next / norm_now)[None, :] * direction
            norm_now = norm_next
    return (solution_field, residual)


def solution(mesh):
    placed = (P(None, ("row", "col")), P(), P(), P(), P(("row", "col"), None))

    def plan(points, lengthscale, noise_var, groups, targets):
        blocks = groups.shape[0]
        square = mesh.shape["row"] == 4 and mesh.shape["col"] in (2, 4, 8, 16)
        whole_field = blocks <= GATHER_LIMIT and blocks == mesh.size and square
        run = gathered_plan if whole_field else per_device
        return run(points, lengthscale, noise_var, groups, targets)

    return jax.shard_map(
        plan,
        mesh=mesh,
        in_specs=placed,
        out_specs=(P(("row", "col"), None), P(("row", "col"), None)),
        check_vma=False,
    )
```

profile of v0, /device:TPU:0, one launch (start us, length us, event | category | flops | bytes accessed | tf_op | source)
XLA Modules:
  0.0 64.9 jit_solution(18333873086594859191)
XLA Ops:
  0.6 0.0 copy-start.5
  0.6 0.0 copy-start
  0.7 0.9 %copy-done = f32[512,128]{1,0:T(8,128)S(1)} copy-done((f32[512,128]{1,0:T(8,128)S(1)}, f32[512,128]{1,0:T(8,128)}, u32[]{:S(2)}) %copy-start) | copy-done | bytes 262168
  1.6 0.0 copy-start.2
  1.6 0.8 %copy-done.2 = f32[16,512]{1,0:T(8,128)S(1)} copy-done((f32[16,512]{1,0:T(8,128)S(1)}, f32[16,512]{1,0:T(8,128)}, u32[]{:S(2)}) %copy-start.2) | copy-done | bytes 32792
  2.4 0.0 copy-start.4
  2.4 0.7 %copy-done.4 = f32[16]{0:T(128)S(1)} copy-done((f32[16]{0:T(128)S(1)}, f32[16]{0:T(128)}, u32[]{:S(2)}) %copy-start.4) | copy-done | bytes 88
  3.0 0.0 copy-start.1
  3.0 19.5 %first_gather.1 = bf16[8,4,48,512]{3,2,1,0:T(8,128)(2,1)S(1)} custom-call(f32[16,512]{1,0:T(8,128)S(1)} %copy-done.2, f32[1,16]{1,0:T(1,128)S(1)} %bitcast.38, f32[512,128]{1,0:T(8,128)S(1)} %copy-done), custom_call_target="tpu_custom_call" | custom-call | tf_op jit(solution)/shard_map/first_gather/pallas_call | solution.py:402
  22.5 0.0 copy-start.3
  22.5 0.6 copy-done.3
  23.2 10.1 %first_product.1 = (bf16[32,512,512]{2,1,0:T(8,128)(2,1)S(1)}, bf16[4,32,512]{2,1,0:T(8,128)(2,1)S(1)}) custom-call(s32[32]{0:T(128)S(1)} %copy-done.3, bf16[32,48,512]{2,1,0:T(8,128)(2,1)S(1)} %bitcast.35), custom_call_target="tpu_custom_call" | custom-call | tf_op jit(solution)/shard_map/first_product/pallas_call | solution.py:425
  33.3 13.2 %second_gather.1 = (bf16[8,4,32,512]{3,2,1,0:T(8,128)(2,1)S(1)}, bf16[4,32,512]{2,1,0:T(8,128)(2,1)S(1)}) custom-call(bf16[4,32,512]{2,1,0:T(8,128)(2,1)S(1)} %get-tuple-element.9.own), custom_call_target="tpu_custom_call" | custom-call | tf_op jit(solution)/shard_map/second_gather/pallas_call | solution.py:435
  46.6 2.9 %second_product.1.own = bf16[4,32,512]{2,1,0:T(8,128)(2,1)S(1)} custom-call(s32[32]{0:T(128)S(1)} %copy-done.3, bf16[32,48,512]{2,1,0:T(8,128)(2,1)S(1)} %bitcast.36, bf16[32,32,512]{2,1,0:T(8,128)(2,1)S(1)} %bitcast.37, bf16[32,512,512]{2,1,0:T(8,128)(2,1)S(1)} %get-tuple-element.11.tiles), custom_call_target="tpu_custom_call" | custom-call | tf_op jit(solution)/shard_map/second_product/pallas_call | solution.py:450
  49.5 0.0 copy-done.1
  49.5 14.4 %finish.1 = (f32[8,128]{1,0:T(8,128)S(1)}, f32[512,128]{1,0:T(8,128)S(1)}, f32[512,128]{1,0:T(8,128)S(1)}) custom-call(bf16[4,32,512]{2,1,0:T(8,128)(2,1)S(1)} %second_product.1.own, bf16[4,32,512]{2,1,0:T(8,128)(2,1)S(1)} %get-tuple-element.12.back, f32[512,128]{1,0:T(8,128)S(1)} %copy-done.1), custom_call_target="tpu_custom_call" | custom-call | tf_op jit(solution)/shard_map/finish/pallas_call | solution.py:460
  64.0 0.0 copy-done.5
  64.0 0.9 %multiply_subtract_fusion = (f32[512,128]{1,0:T(8,128)}, f32[512,128]{1,0:T(8,128)}) fusion(f32[512,128]{1,0:T(8,128)S(1)} %get-tuple-element.15, f32[512,128]{1,0:T(8,128)S(1)} %get-tuple-element.14, f32[512,128]{1,0:T(8,128)S(1)} %copy-done.1, f32[128]{0:T(128)S(1)} %copy-done.5, f32[128]{0:T(128)S(1)} %get-tuple-element.16, f32[128]{0:T(128)S(1)} %bitcast.40, ...), kind=kLoop, calls=%fused_computation | loop fusion | flops 983040 | bytes 1313280 | tf_op jit(solution)/shard_map/sub | solution.py:487
  (2 shorter events, 0.0 us)
Async XLA Ops:
  0.6 63.3 %copy-start.5 = (f32[128]{0:T(128)S(1)}, f32[128]{0:T(128)}, u32[]{:S(2)}) copy-start(f32[128]{0:T(128)} %param.7) | copy-start | bytes 1540
  0.6 1.0 %copy-start = (f32[512,128]{1,0:T(8,128)S(1)}, f32[512,128]{1,0:T(8,128)}, u32[]{:S(2)}) copy-start(f32[512,128]{1,0:T(8,128)} %targets.3) | copy-start | bytes 786436
  1.6 0.8 %copy-start.2 = (f32[16,512]{1,0:T(8,128)S(1)}, f32[16,512]{1,0:T(8,128)}, u32[]{:S(2)}) copy-start(f32[16,512]{1,0:T(8,128)} %points.1) | copy-start | bytes 98308
  2.4 0.7 %copy-start.4 = (f32[16]{0:T(128)S(1)}, f32[16]{0:T(128)}, u32[]{:S(2)}) copy-start(f32[16]{0:T(128)} %param.6) | copy-start | bytes 196
  3.0 46.5 %copy-start.1 = (f32[512,128]{1,0:T(8,128)S(1)}, f32[512,128]{1,0:T(8,128)}, u32[]{:S(2)}) copy-start(f32[512,128]{1,0:T(8,128)} %targets.3) | copy-start | bytes 786436
  22.5 0.7 %copy-start.3 = (s32[32]{0:T(128)S(1)}, s32[32]{0:T(128)}, u32[]{:S(2)}) copy-start(s32[32]{0:T(128)} %groups.3) | copy-start | bytes 388
where the time goes:
time: 65.8 us; the launch traced here: 64.9 us
  Pallas kernels  60.2 us (91%)
  local copies, waits for them, and re-layouts  3.02 us (5%)
  other arithmetic  0.96 us (1%)
  between operations  0.72 us (1%)
    pallas_call x1, Pallas kernels, gathered_plan(): pl.pallas_call(functools.partial(first_gather, n_col), out_shape=jax.Shap...  19.5 us
    pallas_call x1, Pallas kernels, gathered_plan(): pl.pallas_call(functools.partial(finish_kernel, n_col), out_shape=[jax.Sh...  14.4 us
    pallas_call x1, Pallas kernels, gathered_plan(): pl.pallas_call(functools.partial(second_gather, n_col), out_shape=[jax.Sh...  13.2 us
    pallas_call x1, Pallas kernels, gathered_plan(): pl.pallas_call(functools.partial(first_kernel, n_col), out_shape=[jax.Sha...  10.1 us
    unnamed x12, local copies, waits for them, and re-layouts  3.02 us
    pallas_call x1, Pallas kernels, gathered_plan(): pl.pallas_call(functools.partial(second_kernel, n_col), out_shape=slices,...  2.94 us

commit v1 on v0

--- a/solution.py
+++ b/solution.py
@@ -147,7 +147,14 @@
     return groups + ([(2, depth - 2)] if depth > 2 else [])
 
 
-def first_gather(n_col, points, scale, targets, out, own, send_sems, recv_sems, z_sems, own_sem):
+def build_own(coords, spot):
+    left, right = lifted(coords, -2.0, 3, 0).T, lifted(coords, 1.0, 0, 3)
+    for start in range(0, TILE, CHUNK):
+        squared = jnp.dot(left[start:start + CHUNK, :], right, preferred_element_type=jnp.float32)
+        spot[pl.ds(start, CHUNK), :] = wendland(squared)
+
+
+def first_gather(n_col, points, scale, targets, out, diagonal, own, send_sems, recv_sems, z_sems, own_sem):
     plane = Plane(n_col, out, send_sems, recv_sems)
     depth, dims = plane.depth, points.shape[0]
     width = targets.shape[1] // depth
@@ -164,6 +171,13 @@
     for step in range(1, depth):
         plane.launch(own.at[plane.level(depth - step)], out.at[0, step], z_sems.at[step], plane.over_z(step))
     groups = level_groups(depth)
+    last = len(groups) - 1
+
+    def build_group(group):
+        steps = groups[group]
+        for step in range(steps[0], steps[0] + steps[1]):
+            build_own(scaled if step == 0 else out[0, step, pl.ds(width, dims), :], diagonal.at[step])
+
     for group, steps in enumerate(groups):
         if group == 0:
             mine = own.at[pl.ds(plane.z, 1)]
@@ -178,8 +192,10 @@
             plane.second_hop(group - 1, groups[group - 1])
         if group >= 2:
             plane.last_hop(group - 2, groups[group - 2])
-    last = len(groups) - 1
+        if group < last:
+            build_group(group)
     plane.second_hop(last, groups[last])
+    build_group(last)
     for group in range(max(last - 1, 0), last + 1):
         plane.last_hop(group, groups[group])
     keep.wait()
@@ -288,6 +304,8 @@
     count = jnp.int32(0)
     for level in range(depth):
         for block, other in enumerate(labels):
+            if block == level:
+                continue
             order[count] = block * depth + level
             count = count + (other == labels[level]).astype(jnp.int32)
     return count
@@ -312,13 +330,16 @@
     return order[slot] // depth, lax.rem(order[slot], depth)
 
 
-def first_kernel(n_col, groups, gathered, tiles, narrow, order, left, right, spare, image):
+def first_kernel(n_col, groups, gathered, diagonal, tiles, narrow, order, left, right, spare, image):
     width = narrow.shape[1]
     depth, kept = n_col // 2, tiles.shape[0]
     total = find_tiles(n_col, groups, order)
     stored = jnp.minimum(total, kept)
     lift_rows(n_col, width, gathered, right)
-    image[...] = jnp.zeros_like(image)
+    for level in range(depth):
+        image[level] = jnp.dot(
+            gathered[level, pl.ds(0, width), :], diagonal[level], preferred_element_type=jnp.float32
+        )
 
     def one_tile(slot, carry):
         block, level = spot_of(depth, order, slot)
@@ -347,12 +368,13 @@
     narrow[...] = image[...].astype(jnp.bfloat16)
 
 
-def second_kernel(n_col, groups, gathered, source, tiles, narrow, order, left, right, spare, image):
+def second_kernel(n_col, groups, gathered, diagonal, source, tiles, narrow, order, left, right, spare, image):
     width = narrow.shape[1]
     depth, kept = n_col // 2, tiles.shape[0]
     total = find_tiles(n_col, groups, order)
     stored = jnp.minimum(total, kept)
-    image[...] = jnp.zeros_like(image)
+    for level in range(depth):
+        image[level] = jnp.dot(source[level], diagonal[level], preferred_element_type=jnp.float32)
 
     def multiply(slot, tile):
         block, level = spot_of(depth, order, slot)
@@ -399,11 +421,14 @@
             collective_id=number, has_side_effects=True, vmem_limit_bytes=VMEM_LIMIT
         )
 
-    gathered = pl.pallas_call(
+    gathered, diagonal = pl.pallas_call(
         functools.partial(first_gather, n_col),
-        out_shape=jax.ShapeDtypeStruct((8, depth, width + dims, TILE), jnp.bfloat16),
+        out_shape=[
+            jax.ShapeDtypeStruct((8, depth, width + dims, TILE), jnp.bfloat16),
+            jax.ShapeDtypeStruct((depth, TILE, TILE), jnp.bfloat16),
+        ],
         in_specs=[vmem, vmem, vmem],
-        out_specs=vmem,
+        out_specs=[vmem, vmem],
         scratch_shapes=[
             pltpu.VMEM((depth, width + dims, TILE), jnp.bfloat16),
             pltpu.SemaphoreType.DMA((depth - 1 + 14 * parts,)),
@@ -413,7 +438,8 @@
         ],
         compiler_params=remote(0),
         name="first_gather",
-    )(points, scale, targets).reshape(blocks, width + dims, TILE)
+    )(points, scale, targets)
+    gathered = gathered.reshape(blocks, width + dims, TILE)
 
     work = [
         pltpu.SMEM((depth * blocks,), jnp.int32),
@@ -425,12 +451,12 @@
     tiles, first = pl.pallas_call(
         functools.partial(first_kernel, n_col),
         out_shape=[jax.ShapeDtypeStruct((KEPT, TILE, TILE), jnp.bfloat16), slices],
-        in_specs=[smem, vmem],
+        in_specs=[smem, vmem, vmem],
         out_specs=[vmem, vmem],
         scratch_shapes=work,
         compiler_params=pltpu.CompilerParams(vmem_limit_bytes=VMEM_LIMIT),
         name="first_product",
-    )(groups, gathered)
+    )(groups, gathered, diagonal)
 
     source, back = pl.pallas_call(
         functools.partial(second_gather, n_col),
@@ -450,12 +476,12 @@
     second = pl.pallas_call(
         functools.partial(second_kernel, n_col),
         out_shape=slices,
-        in_specs=[smem, vmem, vmem, vmem],
+        in_specs=[smem, vmem, vmem, vmem, vmem],
         out_specs=vmem,
         scratch_shapes=work,
         compiler_params=pltpu.CompilerParams(vmem_limit_bytes=VMEM_LIMIT),
         name="second_product",
-    )(groups, gathered, source.reshape(blocks, width, TILE), tiles)
+    )(groups, gathered, diagonal, source.reshape(blocks, width, TILE), tiles)
 
     total, image, again = pl.pallas_call(
         functools.partial(finish_kernel, n_col),

time: 65.8 us -> 57.3 us (0.87)
  Pallas kernels: 60.2 us -> 52.2 us
    pallas_call x1, Pallas kernels: 10.1 us -> 1.94 us  [gathered_plan(): pl.pallas_call(functools.partial(first_kernel, n_col), out_shape=[jax.Sha...]
    pallas_call x1, Pallas kernels: 13.2 us -> 15.7 us  [gathered_plan(): pl.pallas_call(functools.partial(second_gather, n_col), out_shape=[jax.Sh...]
    pallas_call x1, Pallas kernels: 2.94 us -> 1.22 us  [gathered_plan(): pl.pallas_call(functools.partial(second_kernel, n_col), out_shape=slices,...]
where the time goes in v1:
time: 57.3 us; the launch traced here: 56.9 us
  Pallas kernels  52.2 us (91%)
  local copies, waits for them, and re-layouts  3.02 us (5%)
  other arithmetic  0.96 us (2%)
  between operations  0.73 us (1%)
    pallas_call x1, Pallas kernels, gathered_plan(): pl.pallas_call(functools.partial(first_gather, n_col), out_shape=[jax.Sha...  19.5 us
    pallas_call x1, Pallas kernels, gathered_plan(): pl.pallas_call(functools.partial(second_gather, n_col), out_shape=[jax.Sh...  15.7 us
    pallas_call x1, Pallas kernels, gathered_plan(): pl.pallas_call(functools.partial(finish_kernel, n_col), out_shape=[jax.Sh...  13.8 us
    unnamed x12, local copies, waits for them, and re-layouts  3.02 us
    pallas_call x1, Pallas kernels, gathered_plan(): pl.pallas_call(functools.partial(first_kernel, n_col), out_shape=[jax.Sha...  1.94 us
    pallas_call x1, Pallas kernels, gathered_plan(): pl.pallas_call(functools.partial(second_kernel, n_col), out_shape=slices,...  1.22 us

profile of v1, /device:TPU:0, one launch (start us, length us, event | category | flops | bytes accessed | tf_op | source)
XLA Modules:
  0.0 56.9 jit_solution(1479310739012689662)
XLA Ops:
  0.6 0.0 copy-start
  0.6 0.9 %copy-done = f32[512,128]{1,0:T(8,128)S(1)} copy-done((f32[512,128]{1,0:T(8,128)S(1)}, f32[512,128]{1,0:T(8,128)}, u32[]{:S(2)}) %copy-start) | copy-done | bytes 262168
  1.6 0.0 copy-start.2
  1.6 0.8 %copy-done.2 = f32[16,512]{1,0:T(8,128)S(1)} copy-done((f32[16,512]{1,0:T(8,128)S(1)}, f32[16,512]{1,0:T(8,128)}, u32[]{:S(2)}) %copy-start.2) | copy-done | bytes 32792
  2.3 0.0 copy-start.4
  2.3 0.7 %copy-done.4 = f32[16]{0:T(128)S(1)} copy-done((f32[16]{0:T(128)S(1)}, f32[16]{0:T(128)}, u32[]{:S(2)}) %copy-start.4) | copy-done | bytes 88
  3.0 19.5 %first_gather.1 = (bf16[8,4,48,512]{3,2,1,0:T(8,128)(2,1)S(1)}, bf16[4,512,512]{2,1,0:T(8,128)(2,1)S(1)}) custom-call(f32[16,512]{1,0:T(8,128)S(1)} %copy-done.2, f32[1,16]{1,0:T(1,128)S(1)} %bitcast.38, f32[512,128]{1,0:T(8,128)S(1)} %copy-done), custom_call_target="tpu_custom_call" | custom-call | tf_op jit(solution)/shard_map/first_gather/pallas_call | solution.py:424
  22.5 0.0 copy-start.3
  22.5 0.6 %copy-done.3 = s32[32]{0:T(128)S(1)} copy-done((s32[32]{0:T(128)S(1)}, s32[32]{0:T(128)}, u32[]{:S(2)}) %copy-start.3) | copy-done | bytes 152
  23.2 1.9 %first_product.1 = (bf16[32,512,512]{2,1,0:T(8,128)(2,1)S(1)}, bf16[4,32,512]{2,1,0:T(8,128)(2,1)S(1)}) custom-call(s32[32]{0:T(128)S(1)} %copy-done.3, bf16[32,48,512]{2,1,0:T(8,128)(2,1)S(1)} %bitcast.35, bf16[4,512,512]{2,1,0:T(8,128)(2,1)S(1)} %get-tuple-element.12.diagonal), custom_call_target="tpu_custom_call" | custom-call | tf_op jit(solution)/shard_map/first_product/pallas_call | solution.py:451
  25.1 15.7 %second_gather.1 = (bf16[8,4,32,512]{3,2,1,0:T(8,128)(2,1)S(1)}, bf16[4,32,512]{2,1,0:T(8,128)(2,1)S(1)}) custom-call(bf16[4,32,512]{2,1,0:T(8,128)(2,1)S(1)} %get-tuple-element.13.own), custom_call_target="tpu_custom_call" | custom-call | tf_op jit(solution)/shard_map/second_gather/pallas_call | solution.py:461
  40.8 0.0 copy-start.1
  40.9 0.0 copy-start.5
  40.9 1.2 %second_product.1.own = bf16[4,32,512]{2,1,0:T(8,128)(2,1)S(1)} custom-call(s32[32]{0:T(128)S(1)} %copy-done.3, bf16[32,48,512]{2,1,0:T(8,128)(2,1)S(1)} %bitcast.36, bf16[4,512,512]{2,1,0:T(8,128)(2,1)S(1)} %get-tuple-element.12.diagonal, bf16[32,32,512]{2,1,0:T(8,128)(2,1)S(1)} %bitcast.37, bf16[32,512,512]{2,1,0:T(8,128)(2,1)S(1)} %get-tuple-element.15.tiles), custom_call_target="tpu_custom_call" | custom-call | tf_op jit(solution)/shard_map/second_product/pallas_call | solution.py:476
  42.1 0.0 copy-done.1
  42.1 13.8 %finish.1 = (f32[8,128]{1,0:T(8,128)S(1)}, f32[512,128]{1,0:T(8,128)S(1)}, f32[512,128]{1,0:T(8,128)S(1)}) custom-call(bf16[4,32,512]{2,1,0:T(8,128)(2,1)S(1)} %second_product.1.own, bf16[4,32,512]{2,1,0:T(8,128)(2,1)S(1)} %get-tuple-element.16.back, f32[512,128]{1,0:T(8,128)S(1)} %copy-done.1), custom_call_target="tpu_custom_call" | custom-call | tf_op jit(solution)/shard_map/finish/pallas_call | solution.py:486
  55.9 0.0 copy-done.5
  56.0 0.9 %multiply_subtract_fusion = (f32[512,128]{1,0:T(8,128)}, f32[512,128]{1,0:T(8,128)}) fusion(f32[512,128]{1,0:T(8,128)S(1)} %get-tuple-element.19, f32[512,128]{1,0:T(8,128)S(1)} %get-tuple-element.18, f32[512,128]{1,0:T(8,128)S(1)} %copy-done.1, f32[128]{0:T(128)S(1)} %copy-done.5, f32[128]{0:T(128)S(1)} %get-tuple-element.20, f32[128]{0:T(128)S(1)} %bitcast.40, ...), kind=kLoop, calls=%fused_computation | loop fusion | flops 983040 | bytes 1313280 | tf_op jit(solution)/shard_map/sub | solution.py:513
  (2 shorter events, 0.0 us)
Async XLA Ops:
  0.6 1.0 %copy-start = (f32[512,128]{1,0:T(8,128)S(1)}, f32[512,128]{1,0:T(8,128)}, u32[]{:S(2)}) copy-start(f32[512,128]{1,0:T(8,128)} %targets.3) | copy-start | bytes 786436
  1.6 0.8 %copy-start.2 = (f32[16,512]{1,0:T(8,128)S(1)}, f32[16,512]{1,0:T(8,128)}, u32[]{:S(2)}) copy-start(f32[16,512]{1,0:T(8,128)} %points.1) | copy-start | bytes 98308
  2.3 0.7 %copy-start.4 = (f32[16]{0:T(128)S(1)}, f32[16]{0:T(128)}, u32[]{:S(2)}) copy-start(f32[16]{0:T(128)} %param.6) | copy-start | bytes 196
  22.5 0.7 %copy-start.3 = (s32[32]{0:T(128)S(1)}, s32[32]{0:T(128)}, u32[]{:S(2)}) copy-start(s32[32]{0:T(128)} %groups.3) | copy-start | bytes 388
  40.8 1.3 %copy-start.1 = (f32[512,128]{1,0:T(8,128)S(1)}, f32[512,128]{1,0:T(8,128)}, u32[]{:S(2)}) copy-start(f32[512,128]{1,0:T(8,128)} %targets.3) | copy-start | bytes 786436
  40.9 15.1 %copy-start.5 = (f32[128]{0:T(128)S(1)}, f32[128]{0:T(128)}, u32[]{:S(2)}) copy-start(f32[128]{0:T(128)} %param.7) | copy-start | bytes 1540

commit v2 on v1

--- a/solution.py
+++ b/solution.py
@@ -330,21 +330,21 @@
     return order[slot] // depth, lax.rem(order[slot], depth)
 
 
-def first_kernel(n_col, groups, gathered, diagonal, tiles, narrow, order, left, right, spare, image):
+def first_kernel(n_col, groups, gathered, diagonal, evens, odds, narrow, order, left, right, spare, image):
     width = narrow.shape[1]
-    depth, kept = n_col // 2, tiles.shape[0]
+    depth, kept = n_col // 2, 2 * evens.shape[0]
     total = find_tiles(n_col, groups, order)
     stored = jnp.minimum(total, kept)
+    pairs = stored // 2
     lift_rows(n_col, width, gathered, right)
     for level in range(depth):
         image[level] = jnp.dot(
             gathered[level, pl.ds(0, width), :], diagonal[level], preferred_element_type=jnp.float32
         )
 
-    def one_tile(slot, carry):
+    def make(slot, tile):
         block, level = spot_of(depth, order, slot)
-        build(width, gathered, block, level, left, right, tiles.at[slot])
-        return carry
+        build(width, gathered, block, level, left, right, tile)
 
     def multiply(slot, tile):
         block, level = spot_of(depth, order, slot)
@@ -352,8 +352,23 @@
             gathered[block, pl.ds(0, width), :], tile[...], preferred_element_type=jnp.float32
         )
 
-    def one_stored(slot, carry):
-        multiply(slot, tiles.at[slot])
+    odds[0] = jnp.zeros((TILE, TILE), jnp.bfloat16)
+
+    def one_pair(pair, carry):
+        before = jnp.maximum(pair - 1, 0)
+        make(2 * pair, evens.at[pair])
+        multiply(jnp.maximum(2 * pair - 1, 0), odds.at[before])
+        make(2 * pair + 1, odds.at[pair])
+        multiply(2 * pair, evens.at[pair])
+        return carry
+
+    def single(slot, carry):
+        make(slot, evens.at[pairs])
+        multiply(slot, evens.at[pairs])
+        return carry
+
+    def last_odd(slot, carry):
+        multiply(slot, odds.at[pairs - 1])
         return carry
 
     def one_more(slot, carry):
@@ -362,17 +377,19 @@
         multiply(slot, spare)
         return carry
 
-    lax.fori_loop(0, stored, one_tile, 0)
-    lax.fori_loop(0, stored, one_stored, 0)
+    lax.fori_loop(0, pairs, one_pair, 0)
+    lax.fori_loop(jnp.maximum(2 * pairs - 1, 0), 2 * pairs, last_odd, 0)
+    lax.fori_loop(2 * pairs, stored, single, 0)
     lax.fori_loop(stored, total, one_more, 0)
     narrow[...] = image[...].astype(jnp.bfloat16)
 
 
-def second_kernel(n_col, groups, gathered, diagonal, source, tiles, narrow, order, left, right, spare, image):
+def second_kernel(n_col, groups, gathered, diagonal, source, evens, odds, narrow, order, left, right, spare, image):
     width = narrow.shape[1]
-    depth, kept = n_col // 2, tiles.shape[0]
+    depth, kept = n_col // 2, 2 * evens.shape[0]
     total = find_tiles(n_col, groups, order)
     stored = jnp.minimum(total, kept)
+    pairs = stored // 2
     for level in range(depth):
         image[level] = jnp.dot(source[level], diagonal[level], preferred_element_type=jnp.float32)
 
@@ -380,11 +397,17 @@
         block, level = spot_of(depth, order, slot)
         image[level] += jnp.dot(source[block], tile[...], preferred_element_type=jnp.float32)
 
-    def one_stored(slot, carry):
-        multiply(slot, tiles.at[slot])
+    def one_pair(pair, carry):
+        multiply(2 * pair, evens.at[pair])
+        multiply(2 * pair + 1, odds.at[pair])
         return carry
 
-    lax.fori_loop(0, stored, one_stored, 0)
+    def single(slot, carry):
+        multiply(slot, evens.at[pairs])
+        return carry
+
+    lax.fori_loop(0, pairs, one_pair, 0)
+    lax.fori_loop(2 * pairs, stored, single, 0)
 
     @pl.when(total > kept)
     def _():
@@ -448,11 +471,11 @@
         pltpu.VMEM((TILE, TILE), jnp.bfloat16),
         pltpu.VMEM((depth, width, TILE), jnp.float32),
     ]
-    tiles, first = pl.pallas_call(
+    evens, odds, first = pl.pallas_call(
         functools.partial(first_kernel, n_col),
-        out_shape=[jax.ShapeDtypeStruct((KEPT, TILE, TILE), jnp.bfloat16), slices],
+        out_shape=[jax.ShapeDtypeStruct((KEPT // 2, TILE, TILE), jnp.bfloat16)] * 2 + [slices],
         in_specs=[smem, vmem, vmem],
-        out_specs=[vmem, vmem],
+        out_specs=[vmem, vmem, vmem],
         scratch_shapes=work,
         compiler_params=pltpu.CompilerParams(vmem_limit_bytes=VMEM_LIMIT),
         name="first_product",
@@ -476,12 +499,12 @@
     second = pl.pallas_call(
         functools.partial(second_kernel, n_col),
         out_shape=slices,
-        in_specs=[smem, vmem, vmem, vmem, vmem],
+        in_specs=[smem, vmem, vmem, vmem, vmem, vmem],
         out_specs=vmem,
         scratch_shapes=work,
         compiler_params=pltpu.CompilerParams(vmem_limit_bytes=VMEM_LIMIT),
         name="second_product",
-    )(groups, gathered, diagonal, source.reshape(blocks, width, TILE), tiles)
+    )(groups, gathered, diagonal, source.reshape(blocks, width, TILE), evens, odds)
 
     total, image, again = pl.pallas_call(
         functools.partial(finish_kernel, n_col),

time: 57.3 us -> 54.3 us (0.948); the launches traced: 56.9 us -> 55 us
  Pallas kernels: 52.2 us -> 50.3 us
    pallas_call x1, Pallas kernels: 15.7 us -> 13.3 us  [gathered_plan(): pl.pallas_call(functools.partial(second_gather, n_col), out_shape=[jax.Sh...]
    pallas_call x1, Pallas kernels: 1.94 us -> 2.58 us  [gathered_plan(): pl.pallas_call(functools.partial(first_kernel, n_col), out_shape=[jax.Sha...]
where the time goes in v2:
time: 54.3 us; the launch traced here: 55 us
  Pallas kernels  50.3 us (93%)
  local copies, waits for them, and re-layouts  3.02 us (6%)
  other arithmetic  0.96 us (2%)
  between operations  0.73 us (1%)
    pallas_call x1, Pallas kernels, gathered_plan(): pl.pallas_call(functools.partial(first_gather, n_col), out_shape=[jax.Sha...  19.5 us
    pallas_call x1, Pallas kernels, gathered_plan(): pl.pallas_call(functools.partial(finish_kernel, n_col), out_shape=[jax.Sh...  13.6 us
    pallas_call x1, Pallas kernels, gathered_plan(): pl.pallas_call(functools.partial(second_gather, n_col), out_shape=[jax.Sh...  13.3 us
    unnamed x12, local copies, waits for them, and re-layouts  3.02 us
    pallas_call x1, Pallas kernels, gathered_plan(): pl.pallas_call(functools.partial(first_kernel, n_col), out_shape=[jax.Sha...  2.58 us
    pallas_call x1, Pallas kernels, gathered_plan(): pl.pallas_call(functools.partial(second_kernel, n_col), out_shape=slices,...  1.31 us

profile of v2, /device:TPU:0, one launch (start us, length us, event | category | flops | bytes accessed | tf_op | source)
XLA Modules:
  0.0 55.0 jit_solution(14926061363571869060)
XLA Ops:
  0.6 0.0 copy-start
  0.6 0.9 %copy-done = f32[512,128]{1,0:T(8,128)S(1)} copy-done((f32[512,128]{1,0:T(8,128)S(1)}, f32[512,128]{1,0:T(8,128)}, u32[]{:S(2)}) %copy-start) | copy-done | bytes 262168
  1.6 0.0 copy-start.2
  1.6 0.8 %copy-done.2 = f32[16,512]{1,0:T(8,128)S(1)} copy-done((f32[16,512]{1,0:T(8,128)S(1)}, f32[16,512]{1,0:T(8,128)}, u32[]{:S(2)}) %copy-start.2) | copy-done | bytes 32792
  2.3 0.0 copy-start.4
  2.3 0.7 %copy-done.4 = f32[16]{0:T(128)S(1)} copy-done((f32[16]{0:T(128)S(1)}, f32[16]{0:T(128)}, u32[]{:S(2)}) %copy-start.4) | copy-done | bytes 88
  3.0 19.5 %first_gather.1 = (bf16[8,4,48,512]{3,2,1,0:T(8,128)(2,1)S(1)}, bf16[4,512,512]{2,1,0:T(8,128)(2,1)S(1)}) custom-call(f32[16,512]{1,0:T(8,128)S(1)} %copy-done.2, f32[1,16]{1,0:T(1,128)S(1)} %bitcast.38, f32[512,128]{1,0:T(8,128)S(1)} %copy-done), custom_call_target="tpu_custom_call" | custom-call | tf_op jit(solution)/shard_map/first_gather/pallas_call | solution.py:447
  22.5 0.0 copy-start.3
  22.5 0.6 %copy-done.3 = s32[32]{0:T(128)S(1)} copy-done((s32[32]{0:T(128)S(1)}, s32[32]{0:T(128)}, u32[]{:S(2)}) %copy-start.3) | copy-done | bytes 152
  23.2 2.6 %first_product.1 = (bf16[16,512,512]{2,1,0:T(8,128)(2,1)S(1)}, bf16[16,512,512]{2,1,0:T(8,128)(2,1)S(1)}, bf16[4,32,512]{2,1,0:T(8,128)(2,1)S(1)}) custom-call(s32[32]{0:T(128)S(1)} %copy-done.3, bf16[32,48,512]{2,1,0:T(8,128)(2,1)S(1)} %bitcast.35, bf16[4,512,512]{2,1,0:T(8,128)(2,1)S(1)} %get-tuple-element.13.diagonal), custom_call_target="tpu_custom_call" | custom-call | tf_op jit(solution)/shard_map/first_product/pallas_call | solution.py:474
  25.8 13.3 %second_gather.1 = (bf16[8,4,32,512]{3,2,1,0:T(8,128)(2,1)S(1)}, bf16[4,32,512]{2,1,0:T(8,128)(2,1)S(1)}) custom-call(bf16[4,32,512]{2,1,0:T(8,128)(2,1)S(1)} %get-tuple-element.14.own), custom_call_target="tpu_custom_call" | custom-call | tf_op jit(solution)/shard_map/second_gather/pallas_call | solution.py:484
  39.0 0.0 copy-start.1
  39.0 0.0 copy-start.5
  39.1 1.3 %second_product.1.own = bf16[4,32,512]{2,1,0:T(8,128)(2,1)S(1)} custom-call(s32[32]{0:T(128)S(1)} %copy-done.3, bf16[32,48,512]{2,1,0:T(8,128)(2,1)S(1)} %bitcast.36, bf16[4,512,512]{2,1,0:T(8,128)(2,1)S(1)} %get-tuple-element.13.diagonal, bf16[32,32,512]{2,1,0:T(8,128)(2,1)S(1)} %bitcast.37, bf16[16,512,512]{2,1,0:T(8,128)(2,1)S(1)} %get-tuple-element.16.evens, ...), custom_call_target="tpu_custom_call" | custom-call | tf_op jit(solution)/shard_map/second_product/pallas_call | solution.py:499
  40.4 0.0 copy-done.1
  40.4 13.6 %finish.1 = (f32[8,128]{1,0:T(8,128)S(1)}, f32[512,128]{1,0:T(8,128)S(1)}, f32[512,128]{1,0:T(8,128)S(1)}) custom-call(bf16[4,32,512]{2,1,0:T(8,128)(2,1)S(1)} %second_product.1.own, bf16[4,32,512]{2,1,0:T(8,128)(2,1)S(1)} %get-tuple-element.18.back, f32[512,128]{1,0:T(8,128)S(1)} %copy-done.1), custom_call_target="tpu_custom_call" | custom-call | tf_op jit(solution)/shard_map/finish/pallas_call | solution.py:509
  54.0 0.0 copy-done.5
  54.1 0.9 %multiply_subtract_fusion = (f32[512,128]{1,0:T(8,128)}, f32[512,128]{1,0:T(8,128)}) fusion(f32[512,128]{1,0:T(8,128)S(1)} %get-tuple-element.21, f32[512,128]{1,0:T(8,128)S(1)} %get-tuple-element.20, f32[512,128]{1,0:T(8,128)S(1)} %copy-done.1, f32[128]{0:T(128)S(1)} %copy-done.5, f32[128]{0:T(128)S(1)} %get-tuple-element.22, f32[128]{0:T(128)S(1)} %bitcast.40, ...), kind=kLoop, calls=%fused_computation | loop fusion | flops 983040 | bytes 1313280 | tf_op jit(solution)/shard_map/sub | solution.py:536
  (2 shorter events, 0.0 us)
Async XLA Ops:
  0.6 1.0 %copy-start = (f32[512,128]{1,0:T(8,128)S(1)}, f32[512,128]{1,0:T(8,128)}, u32[]{:S(2)}) copy-start(f32[512,128]{1,0:T(8,128)} %targets.3) | copy-start | bytes 786436
  1.6 0.8 %copy-start.2 = (f32[16,512]{1,0:T(8,128)S(1)}, f32[16,512]{1,0:T(8,128)}, u32[]{:S(2)}) copy-start(f32[16,512]{1,0:T(8,128)} %points.1) | copy-start | bytes 98308
  2.3 0.7 %copy-start.4 = (f32[16]{0:T(128)S(1)}, f32[16]{0:T(128)}, u32[]{:S(2)}) copy-start(f32[16]{0:T(128)} %param.6) | copy-start | bytes 196
  22.5 0.7 %copy-start.3 = (s32[32]{0:T(128)S(1)}, s32[32]{0:T(128)}, u32[]{:S(2)}) copy-start(s32[32]{0:T(128)} %groups.3) | copy-start | bytes 388
  39.0 1.3 %copy-start.1 = (f32[512,128]{1,0:T(8,128)S(1)}, f32[512,128]{1,0:T(8,128)}, u32[]{:S(2)}) copy-start(f32[512,128]{1,0:T(8,128)} %targets.3) | copy-start | bytes 786436
  39.0 15.0 %copy-start.5 = (f32[128]{0:T(128)S(1)}, f32[128]{0:T(128)}, u32[]{:S(2)}) copy-start(f32[128]{0:T(128)} %param.7) | copy-start | bytes 1540
